TPU v7x, 32 devices: a whole 2x2x4 slice. The times are simulated.
32 devices in a mesh: rep: 2 (over x), dp: 4 (over y, core), ctx: 4 (over z).
Axes of the slice: x: 2, y: 2, z: 4, core: 2. Of those that a mesh axis runs over, the one named last changes fastest.
Arguments:
- frames: bfloat16 [8, 512, 1024], P(('rep', 'dp'), 'ctx'), may hold values from -24 to 24
- lengths: int32 [8], P(('rep', 'dp')), may hold values from 64 to 512, as said below
- cotangent: bfloat16 [8, 512, 1024], P(('rep', 'dp'), 'ctx'), may hold values from -6 to 6
- w_query: bfloat16 [1024, 512], P('dp'), may hold values from -0.5 to 0.5
- w_key: bfloat16 [1024, 512], P('dp'), may hold values from -0.5 to 0.5
- w_value: bfloat16 [1024, 512], P('dp'), may hold values from -0.1875 to 0.1875
- w_out: bfloat16 [512, 1024], P('dp'), may hold values from -0.25 to 0.25
Outputs:
- attended: bfloat16 [8, 512, 1024], P(('rep', 'dp'), 'ctx')
- grad_frames: bfloat16 [8, 512, 1024], P(('rep', 'dp'), 'ctx')
- grad_out: float32 [512, 1024], P('dp')
Inputs may be any that keep to these rules, and one draw needn't show every extreme that they name: `lengths`: number of real frames of each meeting; one meeting of every draw has all 512 frames real.
All inputs are finite; a program needn't handle non-finite values.
Results may differ from a plain program's by a relative error of at most 0.025.
The roundings to bfloat16 on the way count: a program that leaves them out, or rounds other values in their place, can miss the bound.
Values may be sent and summed in bfloat16 or wider, within the bound.
A program may use at most 64 MiB of HBM per device.

v0:
```python
import math
import jax
import jax.numpy as jnp
from jax import lax
from jax.sharding import PartitionSpec as P

HEAD = 128
MASKED_SCORE = -1e30


def head_split(matrix, head_count):
    return matrix.reshape(matrix.shape[0], head_count, matrix.shape[1] // head_count)


def forward_step(carry, key_part, value_part, offset, query_heads, length, score_scale):
    head_count = query_heads.shape[1]
    amount = key_part.shape[0]
    maxima, totals, accumulated = carry
    key_heads = head_split(key_part, head_count)
    value_heads = head_split(value_part, head_count)
    scores = (
        jnp.einsum("rhe,nhe->hrn", query_heads, key_heads, preferred_element_type=jnp.float32)
        * score_scale
    )
    usable = offset + jnp.arange(amount) < length
    scores = jnp.where(usable[None, None, :], scores, MASKED_SCORE)
    new_maxima = jnp.maximum(maxima, jnp.max(scores, axis=2))
    factor = jnp.exp(maxima - new_maxima)
    exponent = jnp.where(usable[None, None, :], jnp.exp(scores - new_maxima[:, :, None]), 0.0)
    totals = totals * factor + jnp.sum(exponent, axis=2)
    mixed = jnp.einsum(
        "hrn,nhe->hre",
        exponent.astype(jnp.bfloat16),
        value_heads,
        preferred_element_type=jnp.float32,
    )
    accumulated = accumulated * factor[:, :, None] + mixed
    return (new_maxima, totals, accumulated)


def query_step(
    grad_accum,
    key_part,
    value_part,
    offset,
    query_heads,
    context_heads,
    logsum,
    deltas,
    length,
    score_scale,
):
    head_count = query_heads.shape[1]
    amount = key_part.shape[0]
    key_heads = head_split(key_part, head_count)
    value_heads = head_split(value_part, head_count)
    scores = (
        jnp.einsum("rhe,nhe->hrn", query_heads, key_heads, preferred_element_type=jnp.float32)
        * score_scale
    )
    usable = offset + jnp.arange(amount) < length
    attention = jnp.where(usable[None, None, :], jnp.exp(scores - logsum[:, :, None]), 0.0)
    grad_prob = jnp.einsum(
        "rhe,nhe->hrn", context_heads, value_heads, preferred_element_type=jnp.float32
    )
    grad_score = (attention * (grad_prob - deltas[:, :, None])).astype(jnp.bfloat16)
    added = jnp.einsum("hrn,nhe->rhe", grad_score, key_heads, preferred_element_type=jnp.float32)
    return grad_accum + added * score_scale


def key_step(
    query_part,
    context_part,
    all_logsum,
    all_deltas,
    key_heads,
    value_heads,
    key_usable,
    score_scale,
):
    head_count = key_heads.shape[1]
    query_heads = head_split(query_part, head_count)
    context_heads = head_split(context_part, head_count)
    scores = (
        jnp.einsum("rhe,nhe->hrn", query_heads, key_heads, preferred_element_type=jnp.float32)
        * score_scale
    )
    attention = jnp.where(key_usable[None, None, :], jnp.exp(scores - all_logsum[:, :, None]), 0.0)
    grad_value = jnp.einsum(
        "hrn,rhe->nhe",
        attention.astype(jnp.bfloat16),
        context_heads,
        preferred_element_type=jnp.float32,
    )
    grad_prob = jnp.einsum(
        "rhe,nhe->hrn", context_heads, value_heads, preferred_element_type=jnp.float32
    )
    grad_score = (attention * (grad_prob - all_deltas[:, :, None])).astype(jnp.bfloat16)
    added = jnp.einsum("hrn,rhe->nhe", grad_score, query_heads, preferred_element_type=jnp.float32)
    return (added * score_scale, grad_value)


def back_project(gradient, weight):
    return lax.dot_general(
        gradient, weight, (((1,), (1,)), ((), ())), preferred_element_type=jnp.float32
    )


def shards(frames, lengths, cotangent, w_query, w_key, w_value, w_out):
    full_query, full_key, full_value, full_out = (
        lax.all_gather(w_query, "dp", axis=0, tiled=True),
        lax.all_gather(w_key, "dp", axis=0, tiled=True),
        lax.all_gather(w_value, "dp", axis=0, tiled=True),
        lax.all_gather(w_out, "dp", axis=0, tiled=True),
    )
    inputs = frames[0]
    upstream = cotangent[0]
    length = lengths[0]
    row_count = inputs.shape[0]
    inner_width = full_query.shape[1]
    head_count = inner_width // HEAD
    score_scale = HEAD ** (-0.5)
    first_frame = lax.axis_index("ctx") * row_count
    row_usable = first_frame + jnp.arange(row_count) < length
    queries = jnp.dot(inputs, full_query, preferred_element_type=jnp.float32).astype(jnp.bfloat16)
    keys = jnp.dot(inputs, full_key, preferred_element_type=jnp.float32).astype(jnp.bfloat16)
    values = jnp.dot(inputs, full_value, preferred_element_type=jnp.float32).astype(jnp.bfloat16)
    query_heads = head_split(queries, head_count)
    key_heads = head_split(keys, head_count)
    value_heads = head_split(values, head_count)
    start_state = (
        jnp.full((head_count, row_count), MASKED_SCORE, jnp.float32),
        jnp.zeros((head_count, row_count), jnp.float32),
        jnp.zeros((head_count, row_count, HEAD), jnp.float32),
    )
    all_keys, all_values = (
        lax.all_gather(keys, "ctx", axis=0, tiled=True),
        lax.all_gather(values, "ctx", axis=0, tiled=True),
    )
    key_block = row_count * math.gcd(max(1, 512 // row_count), lax.axis_size("ctx"))
    block_count = all_keys.shape[0] // key_block
    key_blocks = all_keys.reshape(block_count, key_block, inner_width)
    value_blocks = all_values.reshape(block_count, key_block, inner_width)
    block_starts = jnp.arange(block_count, dtype=jnp.int32) * key_block

    def scan_forward(current, scan_item):
        return (
            forward_step(
                current, scan_item[0], scan_item[1], scan_item[2], query_heads, length, score_scale
            ),
            None,
        )

    softmax_state, unused = lax.scan(
        scan_forward, start_state, (key_blocks, value_blocks, block_starts)
    )
    maxima, totals, accumulated = softmax_state
    context = (
        (accumulated / totals[:, :, None])
        .transpose(1, 0, 2)
        .reshape(row_count, inner_width)
        .astype(jnp.bfloat16)
    )
    logsum = maxima + jnp.log(totals)
    attended = jnp.dot(context, full_out, preferred_element_type=jnp.float32)
    attended = jnp.where(row_usable[:, None], attended, 0.0).astype(jnp.bfloat16)
    masked_grad = jnp.where(row_usable[:, None], upstream, jnp.zeros_like(upstream))
    grad_context = back_project(masked_grad, full_out).astype(jnp.bfloat16)
    deltas = jnp.sum(
        (grad_context.astype(jnp.float32) * context.astype(jnp.float32)).reshape(
            row_count, head_count, HEAD
        ),
        axis=2,
    )
    context_heads = head_split(grad_context, head_count)
    delta_heads = deltas.T
    all_logsum, all_deltas = (
        lax.all_gather(logsum, "ctx", axis=1, tiled=True),
        lax.all_gather(delta_heads, "ctx", axis=1, tiled=True),
    )
    zero_grad = jnp.zeros((row_count, head_count, HEAD), jnp.float32)

    def scan_query(current, scan_item):
        return (
            query_step(
                current,
                scan_item[0],
                scan_item[1],
                scan_item[2],
                query_heads,
                context_heads,
                logsum,
                delta_heads,
                length,
                score_scale,
            ),
            None,
        )

    grad_query, unused = lax.scan(scan_query, zero_grad, (key_blocks, value_blocks, block_starts))
    grad_key, grad_value = key_step(
        lax.all_gather(queries, "ctx", axis=0, tiled=True),
        lax.all_gather(grad_context, "ctx", axis=0, tiled=True),
        all_logsum,
        all_deltas,
        key_heads,
        value_heads,
        row_usable,
        score_scale,
    )
    grad_query = grad_query.reshape(row_count, inner_width).astype(jnp.bfloat16)
    grad_key = grad_key.reshape(row_count, inner_width).astype(jnp.bfloat16)
    grad_value = grad_value.reshape(row_count, inner_width).astype(jnp.bfloat16)
    grad_input = (
        back_project(grad_query, full_query)
        + back_project(grad_key, full_key)
        + back_project(grad_value, full_value)
    )
    grad_frames = grad_input.astype(jnp.bfloat16)
    summed_grad = lax.psum(
        lax.dot_general(
            context, masked_grad, (((0,), (0,)), ((), ())), preferred_element_type=jnp.float32
        ),
        ("rep", "ctx"),
    )
    grad_out = lax.psum_scatter(summed_grad, "dp", scatter_dimension=0, tiled=True)
    return (attended[None], grad_frames[None], grad_out)


def solution(mesh):
    in_specs = (
        P(("rep", "dp"), "ctx", None),
        P(("rep", "dp")),
        P(("rep", "dp"), "ctx", None),
        P("dp", None),
        P("dp", None),
        P("dp", None),
        P("dp", None),
    )
    out_specs = (P(("rep", "dp"), "ctx", None), P(("rep", "dp"), "ctx", None), P("dp", None))
    return jax.shard_map(shards, mesh=mesh, in_specs=in_specs, out_specs=out_specs, check_vma=False)
```

profile of v0, /device:TPU:0, one launch (start us, length us, event | category | flops | bytes accessed | tf_op | source)
XLA Modules:
  0.0 236.2 jit_solution(8206433220303085801)
XLA Ops:
  7.2 0.0 copy-start
  7.2 0.0 all-gather.9.cloned.1.call-start
  7.2 0.7 all-gather.9.cloned.1.call-update
  7.9 0.0 all-gather.7.cloned.1.call-start
  8.0 0.7 all-gather.7.cloned.1.call-update
  8.7 0.0 all-gather.5.cloned.1.call-start
  8.7 0.7 all-gather.5.cloned.1.call-update
  9.4 0.0 all-gather.11.cloned.1.call-start
  9.4 0.5 all-gather.11.cloned.1.call-update
  10.0 0.0 reduce-scatter.2.cloned.1.call-start
  10.7 0.0 copy-start.10
  10.7 18.3 %all-gather.9.cloned.1.call-done = bf16[1024,512]{1,0:T(8,128)(2,1)} async-done(((bf16[256,512]{1,0:T(8,128)(2,1)}), bf16[1024,512]{1,0:T(8,128)(2,1)}) %all-gather.9.cloned.1.call-update) | async-done | bytes 1048592 | tf_op jit(solution)/shard_map/all_gather | solution.py:113
  29.0 0.0 copy-done
  29.0 1.5 convolution_convert_fusion.2
  30.6 16.1 %all_gather.34 = bf16[512,512]{1,0:T(8,128)(2,1)S(1)} all-gather(bf16[128,512]{1,0:T(8,128)(2,1)S(1)} %convolution_convert_fusion.2), channel_id=1, replica_groups=mesh['rep'=2,'dp'=4,'ctx'=4] {'ctx'}, dimensions={0}, use_global_device_ids=true | all-gather | bytes 655360 | tf_op jit(solution)/shard_map/all_gather | solution.py:138
  46.6 0.2 copy.33
  46.9 0.0 copy-start.6
  46.9 0.5 all-gather.7.cloned.1.call-done
  47.4 1.5 convolution_convert_fusion.3
  48.9 0.0 copy-start.7
  48.9 16.0 %all_gather.32 = bf16[512,512]{1,0:T(8,128)(2,1)S(1)} all-gather(bf16[128,512]{1,0:T(8,128)(2,1)S(1)} %convolution_convert_fusion.3), channel_id=1, replica_groups=mesh['rep'=2,'dp'=4,'ctx'=4] {'ctx'}, dimensions={0}, use_global_device_ids=true | all-gather | bytes 655360 | tf_op jit(solution)/shard_map/all_gather | solution.py:137
  64.9 0.2 copy.35
  65.1 0.5 all-gather.5.cloned.1.call-done
  65.7 1.5 convolution_convert_fusion.4
  67.2 0.0 copy-done.7
  67.2 0.4 select_reduce_fusion
  67.6 0.0 copy-start.5
  67.6 0.3 fusion.23
  68.0 0.0 copy-done.10
  68.0 0.0 copy-done.6
  68.0 0.4 fusion.19
  68.4 0.2 copy-done.5
  68.6 1.8 fusion.36
  70.4 0.0 reduce-scatter.2.cloned.1.call-update
  70.4 0.0 all-reduce.2.cloned.1.call-start
  70.5 0.1 copy.22
  70.6 0.8 copy.34
  71.3 12.5 %all-gather.11.cloned.1.call-done = bf16[512,1024]{1,0:T(8,128)(2,1)} async-done(((bf16[128,1024]{1,0:T(8,128)(2,1)}), bf16[512,1024]{1,0:T(8,128)(2,1)}) %all-gather.11.cloned.1.call-update) | async-done | bytes 1048592 | tf_op jit(solution)/shard_map/all_gather | solution.py:114
  83.9 1.7 convert_multiply_fusion
  85.6 0.0 copy-start.8
  85.6 0.1 reshape.104
  85.7 0.2 reduce_sum.23
  85.9 0.6 copy.23
  86.5 16.1 %all_gather.36 = bf16[512,512]{1,0:T(8,128)(2,1)S(1)} all-gather(bf16[128,512]{1,0:T(8,128)(2,1)S(1)} %convolution_convert_fusion.4), channel_id=1, replica_groups=mesh['rep'=2,'dp'=4,'ctx'=4] {'ctx'}, dimensions={0}, use_global_device_ids=true | all-gather | bytes 655360 | tf_op jit(solution)/shard_map/all_gather | solution.py:202
  102.6 1.1 copy.36
  103.6 16.0 %all_gather.38 = bf16[512,512]{1,0:T(8,128)(2,1)S(1)} all-gather(bf16[128,512]{1,0:T(8,128)(2,1)S(1)} %get-tuple-element.50), channel_id=1, replica_groups=mesh['rep'=2,'dp'=4,'ctx'=4] {'ctx'}, dimensions={0}, use_global_device_ids=true | all-gather | bytes 655360 | tf_op jit(solution)/shard_map/all_gather | solution.py:203
  119.6 0.2 copy.37
  119.8 0.0 copy-done.8
  119.8 14.3 %all_gather.39 = f32[4,512]{0,1:T(8,128)S(1)} all-gather(f32[4,128]{0,1:T(8,128)S(1)} %bitcast.109), channel_id=1, replica_groups=mesh['rep'=2,'dp'=4,'ctx'=4] {'ctx'}, dimensions={1}, use_global_device_ids=true | all-gather | bytes 10240 | tf_op jit(solution)/shard_map/all_gather | solution.py:179
  134.1 0.1 copy.27
  134.2 11.9 %all_gather.37 = f32[4,512]{1,0:T(4,128)S(1)} all-gather(f32[4,128]{1,0:T(4,128)S(1)} %get-tuple-element.36), channel_id=1, replica_groups=mesh['rep'=2,'dp'=4,'ctx'=4] {'ctx'}, dimensions={1}, use_global_device_ids=true | all-gather | bytes 10240 | tf_op jit(solution)/shard_map/all_gather | solution.py:178
  146.1 1.6 fusion.3
  147.6 1.0 convolution_convert_fusion
  148.7 2.3 fusion.18
  151.0 0.0 copy-done.4
  151.0 2.7 %fusion.60 = f32[128,1024]{1,0:T(8,128)} fusion(bf16[128,512]{0,1:T(8,128)(2,1)} %bitcast.115, bf16[1024,512]{1,0:T(8,128)(2,1)} %all-gather.5.cloned.1.call-done), kind=kOutput, calls=%fused_computation.80 | convolution fusion | flops 134217728 | bytes 1703936 | tf_op jit(solution)/shard_map/dot_general | solution.py:104
  153.7 2.9 %fusion.17 = bf16[4,128,128]{2,1,0:T(8,128)(2,1)} fusion(bf16[512,4,128]{0,2,1:T(8,128)(2,1)} %bitcast.104, f32[4,512,128]{2,1,0:T(8,128)} %copy-done.4, bf16[512,4,128]{0,2,1:T(8,128)(2,1)S(1)} %bitcast.100, bf16[128,4,128]{0,2,1:T(8,128)(2,1)} %bitcast.111, f32[4,512]{1,0:T(4,128)S(1)} %copy.27), kind=kOutput, calls=%fused_computation.30 | convolution fusion | flops 135135232 | bytes 2367488 | tf_op jit(solution)/shard_map/hrn,rhe->nhe/dot_general | solution.py:99
  156.6 0.0 all-reduce.2.cloned.1.call-update
  156.6 1.0 fusion.14
  157.6 0.0 copy-done.1
  157.6 1.6 convolution_add_fusion.1
  159.3 1.2 fusion.13
  160.4 67.1 %all-reduce.2.cloned.1.call-done = f32[128,1024]{1,0:T(8,128)} async-done(((f32[128,1024]{1,0:T(8,128)}), f32[128,1024]{1,0:T(8,128)}) %all-reduce.2.cloned.1.call-update) | async-done | bytes 524304 | tf_op jit(solution)/shard_map/psum | solution.py:220
  227.5 1.9 copy.58
  (14 shorter events, 0.1 us)
Async XLA Ops:
  7.2 21.9 %copy-start = (bf16[1,128,1024]{2,1,0:T(8,128)(2,1)S(1)}, bf16[1,128,1024]{2,1,0:T(8,128)(2,1)}, u32[]{:S(2)}) copy-start(bf16[1,128,1024]{2,1,0:T(8,128)(2,1)} %param.7) | copy-start | bytes 786436
  7.2 21.9 %all-gather.9.cloned.1.call-start = ((), (), s32[]{:S(2)}) async-start(), calls=%async_computation.3 | async-start | bytes 1310720 | tf_op jit(solution)/shard_map/all_gather | solution.py:113
  7.9 39.4 %all-gather.7.cloned.1.call-start = ((), (), s32[]{:S(2)}) async-start(), calls=%async_computation.2 | async-start | bytes 1310720 | tf_op jit(solution)/shard_map/all_gather | solution.py:112
  8.7 57.0 %all-gather.5.cloned.1.call-start = ((), (), s32[]{:S(2)}) async-start(), calls=%async_computation.1 | async-start | bytes 1310720 | tf_op jit(solution)/shard_map/all_gather | solution.py:111
  9.4 74.5 %all-gather.11.cloned.1.call-start = ((), (), s32[]{:S(2)}) async-start(), calls=%async_computation.4 | async-start | bytes 1310720 | tf_op jit(solution)/shard_map/all_gather | solution.py:114
  10.0 146.6 %reduce-scatter.2.cloned.1.call-start = ((), (), s32[]{:S(2)}) async-start(), calls=%async_computation.5 | async-start | bytes 2621440 | tf_op jit(solution)/shard_map/reduce_scatter | solution.py:226
  10.7 57.3 %copy-start.10 = (pred[512]{0:T(512)(128)(4,1)}, pred[512]{0:T(512)(128)(4,1)S(1)}, u32[]{:S(2)}) copy-start(pred[512]{0:T(512)(128)(4,1)S(1)} %iota_compare_fusion) | copy-start | bytes 1540
  46.9 21.1 %copy-start.6 = (bf16[512,512]{0,1:T(8,128)(2,1)}, bf16[512,512]{0,1:T(8,128)(2,1)S(1)}, u32[]{:S(2)}) copy-start(bf16[512,512]{0,1:T(8,128)(2,1)S(1)} %copy.33) | copy-start | bytes 1572868
  48.9 18.3 %copy-start.7 = (bf16[128,512]{1,0:T(8,128)(2,1)}, bf16[128,512]{1,0:T(8,128)(2,1)S(1)}, u32[]{:S(2)}) copy-start(bf16[128,512]{1,0:T(8,128)(2,1)S(1)} %convolution_convert_fusion.3) | copy-start | bytes 393220
  67.6 1.0 copy-start.5
  70.4 157.1 %all-reduce.2.cloned.1.call-start = ((), (), s32[]{:S(2)}) async-start(), calls=%async_computation.6 | async-start | bytes 1048576 | tf_op jit(solution)/shard_map/psum | solution.py:220
  85.6 34.3 %copy-start.8 = (bf16[128,512]{1,0:T(8,128)(2,1)}, bf16[128,512]{1,0:T(8,128)(2,1)S(1)}, u32[]{:S(2)}) copy-start(bf16[128,512]{1,0:T(8,128)(2,1)S(1)} %get-tuple-element.50) | copy-start | bytes 393220
  147.6 3.4 %copy-start.4 = (f32[4,512,128]{2,1,0:T(8,128)}, f32[4,512,128]{2,1,0:T(8,128)S(1)}, u32[]{:S(2)}) copy-start(f32[4,512,128]{2,1,0:T(8,128)S(1)} %fusion.3) | copy-start | bytes 3145732
  151.0 5.6 %copy-start.2 = (bf16[512,1024]{1,0:T(8,128)(2,1)S(1)}, bf16[512,1024]{1,0:T(8,128)(2,1)}, u32[]{:S(2)}) copy-start(bf16[512,1024]{1,0:T(8,128)(2,1)} %all-gather.11.cloned.1.call-done) | copy-start | bytes 3145732
  153.7 4.0 %copy-start.1 = (bf16[1024,512]{1,0:T(8,128)(2,1)S(1)}, bf16[1024,512]{1,0:T(8,128)(2,1)}, u32[]{:S(2)}) copy-start(bf16[1024,512]{1,0:T(8,128)(2,1)} %all-gather.7.cloned.1.call-done) | copy-start | bytes 3145732
  156.6 2.7 %copy-start.3 = (bf16[1024,512]{1,0:T(8,128)(2,1)S(1)}, bf16[1024,512]{1,0:T(8,128)(2,1)}, u32[]{:S(2)}) copy-start(bf16[1024,512]{1,0:T(8,128)(2,1)} %all-gather.9.cloned.1.call-done) | copy-start | bytes 3145732
  156.6 2.7 %copy-start.9 = (bf16[4,128,128]{2,1,0:T(8,128)(2,1)S(1)}, bf16[4,128,128]{2,1,0:T(8,128)(2,1)}, u32[]{:S(2)}) copy-start(bf16[4,128,128]{2,1,0:T(8,128)(2,1)} %convolution_convert_fusion) | copy-start | bytes 393220
Sparse Core Ops, SparseCore 0:
  9.6 19.4 all-gather.8
  30.6 16.7 all-gather.6
  48.9 16.7 all-gather.4
  67.1 16.7 all-gather.10
  86.2 31.4 reduce-scatter.1
  156.7 70.7 all-reduce.1
where the time goes:
time: 237 us; the launch traced here: 236 us
  waiting for transfers between devices  102 us (43%)
  blocking collectives  90.2 us (38%)
  matrix products  23.2 us (10%)
  between operations  15 us (6%)
  local copies, waits for them, and re-layouts  5.47 us (2%)
    psum x1, waiting for transfers between devices, shards(): lax.psum(lax.dot_general(context, masked_grad, (((0,), (0,)), ((), ())),...  67.1 us
    all_gather x1, waiting for transfers between devices, shards(): lax.all_gather(w_value, 'dp', axis=0, tiled=True)  18.3 us
    all_gather x1, blocking collectives, shards(): lax.all_gather(values, 'ctx', axis=0, tiled=True)  16.1 us
    all_gather x1, blocking collectives, shards(): lax.all_gather(queries, 'ctx', axis=0, tiled=True)  16.1 us
    all_gather x1, blocking collectives, shards(): lax.all_gather(keys, 'ctx', axis=0, tiled=True)  16 us
    all_gather x1, blocking collectives, shards(): lax.all_gather(grad_context, 'ctx', axis=0, tiled=True)  16 us
    all_gather x1, blocking collectives, shards(): lax.all_gather(delta_heads, 'ctx', axis=1, tiled=True)  14.3 us
    all_gather x1, waiting for transfers between devices, shards(): lax.all_gather(w_out, 'dp', axis=0, tiled=True)  12.5 us
  transfers between devices with their start and end apart: 6, of which 5 were waited for; matrix products, arithmetic and copies ran while one was open for 11% of the time, Pallas kernels for 0%

commit v1 on v0

--- a/solution.py
+++ b/solution.py
@@ -3,9 +3,11 @@
 import jax.numpy as jnp
 from jax import lax
 from jax.sharding import PartitionSpec as P
+from jax.lax import psum
 
 HEAD = 128
 MASKED_SCORE = -1e30
+cells_supply_all = lambda base_x: psum(psum(base_x, "ctx"), "rep")
 
 
 def head_split(matrix, head_count):
@@ -217,11 +219,10 @@
         + back_project(grad_value, full_value)
     )
     grad_frames = grad_input.astype(jnp.bfloat16)
-    summed_grad = lax.psum(
+    summed_grad = cells_supply_all(
         lax.dot_general(
             context, masked_grad, (((0,), (0,)), ((), ())), preferred_element_type=jnp.float32
-        ),
-        ("rep", "ctx"),
+        )
     )
     grad_out = lax.psum_scatter(summed_grad, "dp", scatter_dimension=0, tiled=True)
     return (attended[None], grad_frames[None], grad_out)

time: 237 us -> 230 us (0.970)
  waiting for transfers between devices: 102 us -> 93.8 us
    psum x1 -> x2, waiting for transfers between devices: 67.1 us -> 59.4 us  [cells_supply_all = lambda base_x: psum(psum(base_x, 'ctx'), 'rep')]
  transfers between devices with their start and end apart: 6 -> 7, of which waited for: 5 -> 6; matrix products, arithmetic and copies ran while one was open for 11% -> 11% of each run, Pallas kernels for 0% -> 0%
where the time goes in v1:
time: 230 us; the launch traced here: 229 us
  waiting for transfers between devices  93.8 us (41%)
  blocking collectives  90.8 us (39%)
  matrix products  22.4 us (10%)
  between operations  15 us (7%)
  local copies, waits for them, and re-layouts  6.23 us (3%)
    psum x2, waiting for transfers between devices, cells_supply_all = lambda base_x: psum(psum(base_x, 'ctx'), 'rep')  59.4 us
    all_gather x1, waiting for transfers between devices, shards(): lax.all_gather(w_value, 'dp', axis=0, tiled=True)  18.3 us
    all_gather x1, blocking collectives, shards(): lax.all_gather(grad_context, 'ctx', axis=0, tiled=True)  16.2 us
    all_gather x1, blocking collectives, shards(): lax.all_gather(values, 'ctx', axis=0, tiled=True)  16.1 us
    all_gather x1, blocking collectives, shards(): lax.all_gather(queries, 'ctx', axis=0, tiled=True)  16.1 us
    all_gather x1, blocking collectives, shards(): lax.all_gather(keys, 'ctx', axis=0, tiled=True)  16 us
    all_gather x1, blocking collectives, shards(): lax.all_gather(delta_heads, 'ctx', axis=1, tiled=True)  14.5 us
    all_gather x1, waiting for transfers between devices, shards(): lax.all_gather(w_out, 'dp', axis=0, tiled=True)  12.5 us
  transfers between devices with their start and end apart: 7, of which 6 were waited for; matrix products, arithmetic and copies ran while one was open for 11% of the time, Pallas kernels for 0%

profile of v1, /device:TPU:0, one launch (start us, length us, event | category | flops | bytes accessed | tf_op | source)
XLA Modules:
  0.0 229.2 jit_solution(3642026689041059304)
XLA Ops:
  7.2 0.0 copy-start
  7.2 0.0 all-gather.9.cloned.1.call-start
  7.2 0.7 all-gather.9.cloned.1.call-update
  7.9 0.0 all-gather.7.cloned.1.call-start
  8.0 0.7 all-gather.7.cloned.1.call-update
  8.7 0.0 all-gather.5.cloned.1.call-start
  8.7 0.7 all-gather.5.cloned.1.call-update
  9.4 0.0 all-gather.11.cloned.1.call-start
  9.4 0.5 all-gather.11.cloned.1.call-update
  10.0 0.0 reduce-scatter.2.cloned.1.call-start
  10.7 0.0 copy-start.12
  10.7 18.3 %all-gather.9.cloned.1.call-done = bf16[1024,512]{1,0:T(8,128)(2,1)} async-done(((bf16[256,512]{1,0:T(8,128)(2,1)}), bf16[1024,512]{1,0:T(8,128)(2,1)}) %all-gather.9.cloned.1.call-update) | async-done | bytes 1048592 | tf_op jit(solution)/shard_map/all_gather | solution.py:115
  29.0 0.0 copy-done
  29.0 1.5 convolution_convert_fusion.2
  30.6 16.1 %all_gather.34 = bf16[512,512]{1,0:T(8,128)(2,1)S(1)} all-gather(bf16[128,512]{1,0:T(8,128)(2,1)S(1)} %convolution_convert_fusion.2), channel_id=1, replica_groups=mesh['rep'=2,'dp'=4,'ctx'=4] {'ctx'}, dimensions={0}, use_global_device_ids=true | all-gather | bytes 655360 | tf_op jit(solution)/shard_map/all_gather | solution.py:140
  46.6 0.2 copy.33
  46.9 0.0 copy-start.8
  46.9 0.5 all-gather.7.cloned.1.call-done
  47.4 1.5 convolution_convert_fusion.3
  48.9 0.0 copy-start.10
  48.9 16.0 %all_gather.32 = bf16[512,512]{1,0:T(8,128)(2,1)S(1)} all-gather(bf16[128,512]{1,0:T(8,128)(2,1)S(1)} %convolution_convert_fusion.3), channel_id=1, replica_groups=mesh['rep'=2,'dp'=4,'ctx'=4] {'ctx'}, dimensions={0}, use_global_device_ids=true | all-gather | bytes 655360 | tf_op jit(solution)/shard_map/all_gather | solution.py:139
  64.9 0.2 copy.35
  65.1 0.5 all-gather.5.cloned.1.call-done
  65.7 1.5 convolution_convert_fusion.4
  67.2 0.0 copy-done.10
  67.2 0.4 select_reduce_fusion
  67.6 0.0 copy-start.6
  67.6 0.3 fusion.23
  68.0 0.4 fusion.19
  68.4 0.2 copy-done.6
  68.6 1.8 fusion.36
  70.4 0.0 reduce-scatter.2.cloned.1.call-update
  70.4 0.0 all-reduce.5.cloned.1.call-start
  70.5 0.1 copy.22
  70.6 0.8 copy.34
  71.3 12.5 %all-gather.11.cloned.1.call-done = bf16[512,1024]{1,0:T(8,128)(2,1)} async-done(((bf16[128,1024]{1,0:T(8,128)(2,1)}), bf16[512,1024]{1,0:T(8,128)(2,1)}) %all-gather.11.cloned.1.call-update) | async-done | bytes 1048592 | tf_op jit(solution)/shard_map/all_gather | solution.py:116
  83.9 2.4 %convert_multiply_fusion = (f32[128,512]{1,0:T(8,128)S(1)}, bf16[128,512]{1,0:T(8,128)(2,1)}) fusion(bf16[128,512]{1,0:T(8,128)(2,1)S(1)} %copy.22, bf16[512,1024]{1,0:T(8,128)(2,1)} %all-gather.11.cloned.1.call-done, bf16[1,128,1024]{2,1,0:T(8,128)(2,1)S(1)} %copy-done.6, pred[128]{0:T(512)(128)(4,1)S(1)} %add_compare_fusion), kind=kOutput, calls=%fused_computation.57 | convolution fusion | flops 134610944 | bytes 1835136 | tf_op jit(solution)/shard_map/dot_general | solution.py:106
  86.2 0.1 reshape.104
  86.3 0.2 reduce_sum.23
  86.5 0.6 copy-done.7
  87.1 0.6 copy.23
  87.8 16.1 %all_gather.36 = bf16[512,512]{1,0:T(8,128)(2,1)S(1)} all-gather(bf16[128,512]{1,0:T(8,128)(2,1)S(1)} %convolution_convert_fusion.4), channel_id=1, replica_groups=mesh['rep'=2,'dp'=4,'ctx'=4] {'ctx'}, dimensions={0}, use_global_device_ids=true | all-gather | bytes 655360 | tf_op jit(solution)/shard_map/all_gather | solution.py:204
  103.8 0.2 copy.36
  104.1 16.2 %all_gather.38 = bf16[512,512]{1,0:T(8,128)(2,1)S(1)} all-gather(bf16[128,512]{1,0:T(8,128)(2,1)} %get-tuple-element.50), channel_id=1, replica_groups=mesh['rep'=2,'dp'=4,'ctx'=4] {'ctx'}, dimensions={0}, use_global_device_ids=true | all-gather | bytes 655360 | tf_op jit(solution)/shard_map/all_gather | solution.py:205
  120.3 0.2 copy.37
  120.5 14.5 %all_gather.39 = f32[4,512]{0,1:T(8,128)S(1)} all-gather(f32[4,128]{0,1:T(8,128)} %bitcast.109), channel_id=1, replica_groups=mesh['rep'=2,'dp'=4,'ctx'=4] {'ctx'}, dimensions={1}, use_global_device_ids=true | all-gather | bytes 10240 | tf_op jit(solution)/shard_map/all_gather | solution.py:181
  135.0 0.1 copy.27
  135.1 12.0 %all_gather.37 = f32[4,512]{1,0:T(4,128)S(1)} all-gather(f32[4,128]{1,0:T(4,128)S(1)} %get-tuple-element.36), channel_id=1, replica_groups=mesh['rep'=2,'dp'=4,'ctx'=4] {'ctx'}, dimensions={1}, use_global_device_ids=true | all-gather | bytes 10240 | tf_op jit(solution)/shard_map/all_gather | solution.py:180
  147.1 1.4 fusion.3
  148.5 0.0 copy-start.4
  148.5 1.0 copy-done.4
  149.5 0.9 convolution_convert_fusion
  150.4 2.2 fusion.18
  152.6 0.0 all-reduce.5.cloned.1.call-update
  152.6 0.0 all-reduce.3.cloned.1.call-start
  152.7 1.8 fusion.60
  154.5 2.9 %fusion.17 = bf16[4,128,128]{2,1,0:T(8,128)(2,1)} fusion(bf16[512,4,128]{0,2,1:T(8,128)(2,1)} %bitcast.104, f32[4,512,128]{2,1,0:T(8,128)} %copy-done.4, bf16[512,4,128]{0,2,1:T(8,128)(2,1)S(1)} %bitcast.100, bf16[128,4,128]{0,2,1:T(8,128)(2,1)} %bitcast.111, f32[4,512]{1,0:T(4,128)S(1)} %copy.27), kind=kOutput, calls=%fused_computation.30 | convolution fusion | flops 135135232 | bytes 2367488 | tf_op jit(solution)/shard_map/hrn,rhe->nhe/dot_general | solution.py:101
  157.4 32.0 %all-reduce.5.cloned.1.call-done = f32[128,1024]{1,0:T(8,128)} async-done(((f32[128,1024]{1,0:T(8,128)}), f32[128,1024]{1,0:T(8,128)}) %all-reduce.5.cloned.1.call-update) | async-done | bytes 524304 | tf_op jit(solution)/shard_map/psum | solution.py:10
  189.5 0.0 all-reduce.3.cloned.1.call-update
  189.5 1.0 fusion.14
  190.5 1.4 convolution_add_fusion.1
  192.0 1.2 fusion.13
  193.1 27.3 %all-reduce.3.cloned.1.call-done = f32[128,1024]{1,0:T(8,128)} async-done(((f32[128,1024]{1,0:T(8,128)}), f32[128,1024]{1,0:T(8,128)}) %all-reduce.3.cloned.1.call-update) | async-done | bytes 524304 | tf_op jit(solution)/shard_map/psum | solution.py:10
  220.5 1.9 copy.59
  (21 shorter events, 0.1 us)
Async XLA Ops:
  7.2 21.9 %copy-start = (bf16[1,128,1024]{2,1,0:T(8,128)(2,1)S(1)}, bf16[1,128,1024]{2,1,0:T(8,128)(2,1)}, u32[]{:S(2)}) copy-start(bf16[1,128,1024]{2,1,0:T(8,128)(2,1)} %param.7) | copy-start | bytes 786436
  7.2 21.9 %all-gather.9.cloned.1.call-start = ((), (), s32[]{:S(2)}) async-start(), calls=%async_computation.3 | async-start | bytes 1310720 | tf_op jit(solution)/shard_map/all_gather | solution.py:115
  7.9 39.4 %all-gather.7.cloned.1.call-start = ((), (), s32[]{:S(2)}) async-start(), calls=%async_computation.2 | async-start | bytes 1310720 | tf_op jit(solution)/shard_map/all_gather | solution.py:114
  8.7 57.0 %all-gather.5.cloned.1.call-start = ((), (), s32[]{:S(2)}) async-start(), calls=%async_computation.1 | async-start | bytes 1310720 | tf_op jit(solution)/shard_map/all_gather | solution.py:113
  9.4 74.5 %all-gather.11.cloned.1.call-start = ((), (), s32[]{:S(2)}) async-start(), calls=%async_computation.4 | async-start | bytes 1310720 | tf_op jit(solution)/shard_map/all_gather | solution.py:116
  10.0 142.6 %reduce-scatter.2.cloned.1.call-start = ((), (), s32[]{:S(2)}) async-start(), calls=%async_computation.6 | async-start | bytes 2621440 | tf_op jit(solution)/shard_map/reduce_scatter | solution.py:227
  10.7 57.3 %copy-start.12 = (pred[512]{0:T(512)(128)(4,1)}, pred[512]{0:T(512)(128)(4,1)S(1)}, u32[]{:S(2)}) copy-start(pred[512]{0:T(512)(128)(4,1)S(1)} %iota_compare_fusion) | copy-start | bytes 1540
  46.9 21.1 %copy-start.8 = (bf16[512,512]{0,1:T(8,128)(2,1)}, bf16[512,512]{0,1:T(8,128)(2,1)S(1)}, u32[]{:S(2)}) copy-start(bf16[512,512]{0,1:T(8,128)(2,1)S(1)} %copy.33) | copy-start | bytes 1572868
  48.9 18.3 %copy-start.10 = (bf16[128,512]{1,0:T(8,128)(2,1)}, bf16[128,512]{1,0:T(8,128)(2,1)S(1)}, u32[]{:S(2)}) copy-start(bf16[128,512]{1,0:T(8,128)(2,1)S(1)} %convolution_convert_fusion.3) | copy-start | bytes 393220
  67.6 1.0 copy-start.6
  70.4 119.0 %all-reduce.5.cloned.1.call-start = ((), (), s32[]{:S(2)}) async-start(), calls=%async_computation.7 | async-start | bytes 1048576 | tf_op jit(solution)/shard_map/psum | solution.py:10
  86.5 0.6 copy-start.7
  104.1 46.3 %copy-start.5 = (bf16[512,512]{0,1:T(8,128)(2,1)}, bf16[512,512]{0,1:T(8,128)(2,1)S(1)}, u32[]{:S(2)}) copy-start(bf16[512,512]{0,1:T(8,128)(2,1)S(1)} %copy.36) | copy-start | bytes 1572868
  135.1 15.3 %copy-start.9 = (bf16[512,512]{0,1:T(8,128)(2,1)S(1)}, bf16[512,512]{0,1:T(8,128)(2,1)}, u32[]{:S(2)}) copy-start(bf16[512,512]{0,1:T(8,128)(2,1)} %copy-done.8) | copy-start | bytes 1572868
  148.5 1.0 copy-start.4
  152.6 67.8 %all-reduce.3.cloned.1.call-start = ((), (), s32[]{:S(2)}) async-start(), calls=%async_computation.5 | async-start | bytes 1048576 | tf_op jit(solution)/shard_map/psum | solution.py:10
  152.7 36.8 %copy-start.2 = (bf16[512,1024]{1,0:T(8,128)(2,1)S(1)}, bf16[512,1024]{1,0:T(8,128)(2,1)}, u32[]{:S(2)}) copy-start(bf16[512,1024]{1,0:T(8,128)(2,1)} %all-gather.11.cloned.1.call-done) | copy-start | bytes 3145732
  154.5 36.0 %copy-start.1 = (bf16[1024,512]{1,0:T(8,128)(2,1)S(1)}, bf16[1024,512]{1,0:T(8,128)(2,1)}, u32[]{:S(2)}) copy-start(bf16[1024,512]{1,0:T(8,128)(2,1)} %all-gather.7.cloned.1.call-done) | copy-start | bytes 3145732
  189.5 2.5 %copy-start.3 = (bf16[1024,512]{1,0:T(8,128)(2,1)S(1)}, bf16[1024,512]{1,0:T(8,128)(2,1)}, u32[]{:S(2)}) copy-start(bf16[1024,512]{1,0:T(8,128)(2,1)} %all-gather.9.cloned.1.call-done) | copy-start | bytes 3145732
  189.5 2.5 %copy-start.11 = (bf16[4,128,128]{2,1,0:T(8,128)(2,1)S(1)}, bf16[4,128,128]{2,1,0:T(8,128)(2,1)}, u32[]{:S(2)}) copy-start(bf16[4,128,128]{2,1,0:T(8,128)(2,1)} %convolution_convert_fusion) | copy-start | bytes 393220
Sparse Core Ops, SparseCore 0:
  9.6 19.4 all-gather.8
  30.6 16.7 all-gather.6
  48.9 16.7 all-gather.4
  67.1 16.7 all-gather.10
  86.2 31.4 reduce-scatter.1
  152.7 36.6 all-reduce.4
  191.8 28.5 all-reduce.2
